TPU v7x, 32 devices: a whole 2x2x4 slice. The times are simulated.
32 devices in a mesh: row: 8 (over y, x, core), col: 4 (over z).
Axes of the slice: x: 2, y: 2, z: 4, core: 2. Of those that a mesh axis runs over, the one named last changes fastest.
Arguments:
- inputs: bfloat16 [192, 12288], P('row', 'col'), may hold values from -6 to 6
- w_in: bfloat16 [12288, 24576], P('col', 'row'), may hold values from -0.0546875 to 0.0546875
- w_out: bfloat16 [24576, 12288], P('row', 'col'), may hold values from -0.0390625 to 0.0390625
- out_grad: bfloat16 [192, 12288], P('row', 'col'), may hold values from -6 to 6
Outputs:
- output: bfloat16 [192, 12288], P('row', 'col')
- input_grad: bfloat16 [192, 12288], P('row', 'col')
- grad_in_w: bfloat16 [12288, 24576], P('col', 'row')
- grad_out_w: bfloat16 [24576, 12288], P('row', 'col')
All inputs are finite; a program needn't handle non-finite values.
Results may differ from a plain program's by a relative error of at most 0.0049.
Values may be sent and summed in bfloat16 or wider, within the bound.
A program may use at most 128 MiB of HBM per device.

v0:
```python
import jax
import jax.numpy as jnp
from jax import lax
from jax.sharding import PartitionSpec as P

gelu_scale = 0.7978845608028654
gelu_cubic = 0.044715


def gelu_parts(hidden):
    inner = gelu_scale * (hidden + gelu_cubic * hidden * hidden * hidden)
    tangent = jnp.tanh(inner)
    value = 0.5 * hidden * (1.0 + tangent)
    slopes = 0.5 * (1.0 + tangent) + 0.5 * hidden * (1.0 - tangent * tangent) * gelu_scale * (
        1.0 + 3.0 * gelu_cubic * hidden * hidden
    )
    return (value, slopes)


def contract_first(left, right):
    return lax.dot_general(
        left, right, (((0,), (0,)), ((), ())), preferred_element_type=jnp.float32
    )


def contract_last(left, right):
    return lax.dot_general(
        left, right, (((1,), (1,)), ((), ())), preferred_element_type=jnp.float32
    )


def local(inputs, w_in, w_out, out_grad):
    all_inputs, all_grads = (
        lax.all_gather(inputs, "row", axis=0, tiled=True),
        lax.all_gather(out_grad, "row", axis=0, tiled=True),
    )
    hidden_part = jnp.dot(all_inputs, w_in, preferred_element_type=jnp.float32)
    act_part = contract_last(all_grads, w_out)
    hidden = lax.psum(hidden_part, "col")
    value, slopes = gelu_parts(hidden)
    activation = value.astype(jnp.bfloat16)
    act_grad = lax.psum(act_part, "col")
    hid_grad = (act_grad * slopes).astype(jnp.bfloat16)
    grad_out_w = contract_first(activation, all_grads).astype(jnp.bfloat16)
    grad_in_w = contract_first(all_inputs, hid_grad).astype(jnp.bfloat16)
    picked = activation
    output = lax.psum_scatter(
        jnp.dot(picked, w_out, preferred_element_type=jnp.float32),
        "row",
        scatter_dimension=0,
        tiled=True,
    )
    picked = hid_grad
    input_grad = lax.psum_scatter(
        contract_last(picked, w_in), "row", scatter_dimension=0, tiled=True
    )
    return (output.astype(jnp.bfloat16), input_grad.astype(jnp.bfloat16), grad_in_w, grad_out_w)


def solution(mesh):
    placed = (P("row", "col"), P("col", "row"), P("row", "col"), P("row", "col"))
    return jax.shard_map(
        local,
        mesh=mesh,
        in_specs=placed,
        out_specs=(P("row", "col"), P("row", "col"), P("col", "row"), P("row", "col")),
        check_vma=False,
    )
```

profile of v0, /device:TPU:0, one launch (start us, length us, event | category | flops | bytes accessed | tf_op | source)
XLA Modules:
  0.0 358.1 jit_solution(4976762169256026040)
XLA Ops:
  7.2 0.0 all-gather.3.cloned.1.call-start
  7.2 0.7 all-gather.3.cloned.1.call-update
  7.9 0.0 all-gather.5.cloned.1.call-start
  7.9 0.7 all-gather.5.cloned.1.call-update
  8.6 0.0 all-reduce.3.cloned.1.call-start
  8.7 28.0 %all-gather.3.cloned.1.call-done = bf16[192,3072]{1,0:T(8,128)(2,1)} async-done(((bf16[24,3072]{1,0:T(8,128)(2,1)}), bf16[192,3072]{1,0:T(8,128)(2,1)}) %all-gather.3.cloned.1.call-update) | async-done | bytes 1179664 | tf_op jit(solution)/shard_map/all_gather | solution.py:34
  36.7 12.0 %fusion.8 = f32[192,3072]{1,0:T(8,128)} fusion(bf16[192,3072]{1,0:T(8,128)(2,1)} %all-gather.3.cloned.1.call-done, bf16[3072,3072]{1,0:T(8,128)(2,1)} %param.5), kind=kOutput, calls=%fused_computation.13 | convolution fusion | flops 3623878656 | bytes 22413312 | tf_op jit(solution)/shard_map/dot_general | solution.py:37
  48.6 14.0 %all-gather.5.cloned.1.call-done = bf16[192,3072]{1,0:T(8,128)(2,1)} async-done(((bf16[24,3072]{1,0:T(8,128)(2,1)}), bf16[192,3072]{1,0:T(8,128)(2,1)}) %all-gather.5.cloned.1.call-update) | async-done | bytes 1179664 | tf_op jit(solution)/shard_map/all_gather | solution.py:35
  62.7 14.5 %fusion.9 = f32[192,3072]{1,0:T(8,128)} fusion(bf16[192,3072]{1,0:T(8,128)(2,1)} %all-gather.5.cloned.1.call-done, bf16[3072,3072]{1,0:T(8,128)(2,1)} %param.6), kind=kOutput, calls=%fused_computation.14 | convolution fusion | flops 3623878656 | bytes 22413312 | tf_op jit(solution)/shard_map/dot_general | solution.py:27
  77.2 0.0 all-reduce.3.cloned.1.call-update
  77.2 0.0 reduce-scatter.3.cloned.1.call-start
  77.2 172.4 %all-reduce.3.cloned.1.call-done = (f32[192,3072]{1,0:T(8,128)}, f32[192,3072]{1,0:T(8,128)}) async-done(((f32[192,3072]{1,0:T(8,128)}, f32[192,3072]{1,0:T(8,128)}), (f32[192,3072]{1,0:T(8,128)}, f32[192,3072]{1,0:T(8,128)})) %all-reduce.3.cloned.1.call-update) | async-done | bytes 4718608 | tf_op jit(solution)/shard_map/psum | solution.py:39
  249.6 12.6 %fusion.7 = f32[192,3072]{1,0:T(8,128)} fusion(bf16[3072,3072]{1,0:T(8,128)(2,1)} %param.6, f32[192,3072]{1,0:T(8,128)} %get-tuple-element.8), kind=kOutput, calls=%fused_computation.12 | convolution fusion | flops 3629187072 | bytes 23592960 | tf_op jit(solution)/shard_map/dot_general | solution.py:48
  262.2 0.0 copy-start
  262.2 0.0 reduce-scatter.3.cloned.1.call-update
  262.2 0.2 reduce-scatter.5.cloned.1.call-start
  262.5 1.4 copy-done
  263.9 3.1 fusion.6
  267.0 12.0 %fusion.10 = f32[192,3072]{1,0:T(8,128)} fusion(bf16[192,3072]{1,0:T(8,128)(2,1)S(1)} %fusion.6, bf16[3072,3072]{1,0:T(8,128)(2,1)} %param.5), kind=kOutput, calls=%fused_computation.15 | convolution fusion | flops 3623878656 | bytes 22413312 | tf_op jit(solution)/shard_map/dot_general | solution.py:27
  279.0 0.0 reduce-scatter.5.cloned.1.call-update
  279.0 10.8 %convert_bitcast_fusion = bf16[3072,3072]{0,1:T(8,128)(2,1)} fusion(bf16[192,3072]{1,0:T(8,128)(2,1)S(1)} %fusion.6, bf16[192,3072]{1,0:T(8,128)(2,1)} %all-gather.3.cloned.1.call-done), kind=kOutput, calls=%fused_computation | convolution fusion | flops 3633315840 | bytes 21233664 | tf_op jit(solution)/shard_map/dot_general | solution.py:21
  289.9 0.0 copy-start.1
  289.9 24.7 %copy.8 = bf16[3072,3072]{1,0:T(8,128)(2,1)} copy(bf16[3072,3072]{0,1:T(8,128)(2,1)} %convert_bitcast_fusion) | data formatting | bytes 37748736
  314.6 0.0 copy-done.1
  314.6 9.6 %convolution_convert_fusion = bf16[3072,3072]{1,0:T(8,128)(2,1)} fusion(bf16[192,3072]{1,0:T(8,128)(2,1)S(1)} %copy-done.1, f32[192,3072]{1,0:T(8,128)S(1)} %copy-done), kind=kOutput, calls=%fused_computation.1 | convolution fusion | flops 3638624256 | bytes 22413312 | tf_op jit(solution)/shard_map/dot_general | solution.py:21
  324.2 0.0 reduce-scatter.3.cloned.1.call-done
  324.2 1.6 convert_element_type.22
  325.8 24.2 %reduce-scatter.5.cloned.1.call-done = f32[24,3072]{1,0:T(8,128)} async-done(((f32[192,3072]{1,0:T(8,128)}), f32[24,3072]{1,0:T(8,128)}) %reduce-scatter.5.cloned.1.call-update) | async-done | bytes 294928 | tf_op jit(solution)/shard_map/reduce_scatter | solution.py:54
  350.0 1.6 convert_element_type.24
Async XLA Ops:
  7.2 29.5 %all-gather.3.cloned.1.call-start = ((), (), s32[]{:S(2)}) async-start(), calls=%async_computation.2 | async-start | bytes 1327104 | tf_op jit(solution)/shard_map/all_gather | solution.py:34
  7.9 54.8 %all-gather.5.cloned.1.call-start = ((), (), s32[]{:S(2)}) async-start(), calls=%async_computation.4 | async-start | bytes 1327104 | tf_op jit(solution)/shard_map/all_gather | solution.py:35
  8.6 241.0 %all-reduce.3.cloned.1.call-start = ((), (), s32[]{:S(2)}) async-start(), calls=%async_computation.6 | async-start | bytes 9437184 | tf_op jit(solution)/shard_map/psum | solution.py:39
  77.2 247.0 %reduce-scatter.3.cloned.1.call-start = ((), (), s32[]{:S(2)}) async-start(), calls=%async_computation.3 | async-start | bytes 2654208 | tf_op jit(solution)/shard_map/reduce_scatter | solution.py:47
  262.2 1.7 copy-start
  262.2 87.7 %reduce-scatter.5.cloned.1.call-start = ((), (), s32[]{:S(2)}) async-start(), calls=%async_computation.5 | async-start | bytes 2654208 | tf_op jit(solution)/shard_map/reduce_scatter | solution.py:54
  289.9 24.7 %copy-start.1 = (bf16[192,3072]{1,0:T(8,128)(2,1)S(1)}, bf16[192,3072]{1,0:T(8,128)(2,1)}, u32[]{:S(2)}) copy-start(bf16[192,3072]{1,0:T(8,128)(2,1)} %all-gather.5.cloned.1.call-done) | copy-start | bytes 3538948
Sparse Core Ops, SparseCore 0:
  9.9 26.7 all-gather.2
  38.6 24.0 all-gather.4
  77.3 172.2 all-reduce.2
  262.4 41.5 reduce-scatter.2
  307.5 42.4 reduce-scatter.4
where the time goes:
time: 359 us; the launch traced here: 358 us
  waiting for transfers between devices  240 us (67%)
  matrix products  71.4 us (20%)
  local copies, waits for them, and re-layouts  26.2 us (7%)
  between operations  13.8 us (4%)
  other arithmetic  6.42 us (2%)
    psum x1, waiting for transfers between devices, local(): hidden = lax.psum(hidden_part, 'col')  172 us
    all_gather x1, waiting for transfers between devices, local(): lax.all_gather(inputs, 'row', axis=0, tiled=True)  28 us
    dot_general x2, matrix products, contract_last(): lax.dot_general(left, right, (((1,), (1,)), ((), ())), preferred_element_...  26.5 us
    unnamed x5, local copies, waits for them, and re-layouts  26.2 us
    reduce_scatter x1, waiting for transfers between devices, local(): lax.psum_scatter(contract_last(picked, w_in), 'row', scatter_dimension=0,...  24.2 us
    dot_general x2, matrix products, contract_first(): lax.dot_general(left, right, (((0,), (0,)), ((), ())), preferred_element_...  20.4 us
    all_gather x1, waiting for transfers between devices, local(): lax.all_gather(out_grad, 'row', axis=0, tiled=True)  14 us
    dot_general x1, matrix products, local(): jnp.dot(picked, w_out, preferred_element_type=jnp.float32)  12.6 us
  transfers between devices with their start and end apart: 5, of which 4 were waited for; matrix products, arithmetic and copies ran while one was open for 21% of the time, Pallas kernels for 0%

commit v1 on v0

v1 whole, which is shorter than its diff:
```python
import functools

import jax
import jax.numpy as jnp
from jax import lax
from jax.experimental import pallas as pl
from jax.experimental.pallas import tpu as pltpu
from jax.sharding import PartitionSpec as P

gelu_scale = 0.7978845608028654
gelu_cubic = 0.044715
MESH = pl.DeviceIdType.MESH
CHUNK = 256
f32, bf16 = jnp.float32, jnp.bfloat16


def gelu_parts(hidden):
    inner = gelu_scale * (hidden + gelu_cubic * hidden * hidden * hidden)
    tangent = jnp.tanh(inner)
    value = 0.5 * hidden * (1.0 + tangent)
    slopes = 0.5 * (1.0 + tangent) + 0.5 * hidden * (1.0 - tangent * tangent) * gelu_scale * (
        1.0 + 3.0 * gelu_cubic * hidden * hidden
    )
    return (value, slopes)


def contract_first(left, right):
    return lax.dot_general(left, right, (((0,), (0,)), ((), ())), preferred_element_type=f32)


def contract_last(left, right):
    return lax.dot_general(left, right, (((1,), (1,)), ((), ())), preferred_element_type=f32)


def layer_kernel(
    rows, cols, own_in, own_grad, w_in, w_out,
    x, og, act, hg, out_acc, ig_acc,
    slab, win, wout, from_outer, from_inner, to_inner, kept,
    gather_send, gather_recv, share_send, w_sem, outer_sem, inner_sem, in_send, out_send,
):
    row, col = lax.axis_index("row"), lax.axis_index("col")
    chips, half = rows // 2, cols // 2
    chip, core = row // 2, row % 2
    sibling = chip * 2 + (1 - core)
    chunks, tokens = win.shape[0], own_in.shape[0]

    lower = col < half
    inner = jnp.where(lower, col + 1, col - 1)
    outer = jnp.where(lower, col - 1, col + 1)
    away = jnp.where(lower, half - 1 - col, col - half)
    is_mid = away == 0
    has_outer = away < half - 1

    def weight_copies(j):
        cut = pl.ds(pl.multiple_of(j * CHUNK, CHUNK), CHUNK)
        return (
            pltpu.make_async_copy(w_in.at[:, cut], win.at[j], w_sem.at[0, j]),
            pltpu.make_async_copy(w_out.at[cut, :], wout.at[j], w_sem.at[1, j]),
        )

    @pl.loop(0, chunks)
    def _(j):
        for copy in weight_copies(j):
            copy.start()

    barrier = pltpu.get_barrier_semaphore()
    for k in range(1, chips):
        there = lax.rem(chip + k, chips) * 2 + core
        pl.semaphore_signal(barrier, inc=1, device_id=(there, col), device_id_type=MESH)
    pl.semaphore_signal(barrier, inc=1, device_id=(sibling, col), device_id_type=MESH)
    pl.semaphore_signal(barrier, inc=1, device_id=(row, inner), device_id_type=MESH)

    @pl.when(has_outer)
    def _():
        pl.semaphore_signal(barrier, inc=1, device_id=(row, outer), device_id_type=MESH)
        pl.semaphore_wait(barrier, chips + 2)

    @pl.when(jnp.logical_not(has_outer))
    def _():
        pl.semaphore_wait(barrier, chips + 1)

    own = (own_in, own_grad)

    def send_block(a, k):
        there = lax.rem(chip + k, chips) * 2 + core
        return pltpu.make_async_remote_copy(
            src_ref=own[a], dst_ref=slab.at[a, row], send_sem=gather_send.at[a, k],
            recv_sem=gather_recv.at[a, row], device_id=(there, col), device_id_type=MESH,
        )

    def share_block(a, k):
        source = lax.rem(chip + chips - k, chips) * 2 + core
        return pltpu.make_async_remote_copy(
            src_ref=own[a] if k == 0 else slab.at[a, source], dst_ref=slab.at[a, source],
            send_sem=share_send.at[a, k], recv_sem=gather_recv.at[a, source],
            device_id=(sibling, col), device_id_type=MESH,
        )

    def arrived(a, source):
        pltpu.make_async_remote_copy(
            src_ref=own[a], dst_ref=slab.at[a, source], send_sem=gather_send.at[a, 0],
            recv_sem=gather_recv.at[a, source], device_id=(sibling, col), device_id_type=MESH,
        ).wait_recv()

    for a in range(2):
        for k in range(1, chips):
            send_block(a, k).start()
        share_block(a, 0).start()
    for a, (whole, wide) in enumerate(((x, out_acc), (og, ig_acc))):
        for k in range(1, chips):
            arrived(a, lax.rem(chip + chips - k, chips) * 2 + core)
            share_block(a, k).start()
        for k in range(chips):
            arrived(a, lax.rem(chip + chips - k, chips) * 2 + 1 - core)

        def unfold(r, _, a=a, wide=wide):
            at = pl.ds(pl.multiple_of(r * tokens, 8), tokens)

            @pl.when(r == row)
            def _():
                wide[at, :] = own[a][...].astype(f32)

            @pl.when(r != row)
            def _():
                wide[at, :] = slab[a, r].astype(f32)

        lax.fori_loop(0, rows, unfold, None)
        whole[...] = wide[...].astype(bf16)
        wide[...] = jnp.zeros_like(wide)

    def sum_copy(j):
        return pltpu.make_async_remote_copy(
            src_ref=to_inner.at[j], dst_ref=from_outer.at[j], send_sem=in_send.at[j],
            recv_sem=outer_sem.at[j], device_id=(row, inner), device_id_type=MESH,
        )

    def middle_copy(j):
        return pltpu.make_async_remote_copy(
            src_ref=to_inner.at[j], dst_ref=from_inner.at[j], send_sem=in_send.at[j],
            recv_sem=inner_sem.at[j], device_id=(row, inner), device_id_type=MESH,
        )

    def result_copy(j):
        return pltpu.make_async_remote_copy(
            src_ref=from_inner.at[j], dst_ref=from_inner.at[j], send_sem=out_send.at[j],
            recv_sem=inner_sem.at[j], device_id=(row, outer), device_id_type=MESH,
        )

    lag = 1 + 3 * away

    def step(s, _):
        @pl.when(s < chunks)
        def _():
            for copy in weight_copies(s):
                copy.wait()
            slot = lax.rem(s, 2)
            kept[slot, 0] = jnp.dot(x[...], win[s], preferred_element_type=f32)
            kept[slot, 1] = contract_last(og[...], wout[s])

            @pl.when(has_outer)
            def _():
                sum_copy(s).wait_recv()
                kept[slot] = kept[slot] + from_outer[s].astype(f32)

            to_inner[s] = kept[slot].astype(bf16)

            @pl.when(is_mid)
            def _():
                middle_copy(s).start()

            @pl.when(jnp.logical_not(is_mid))
            def _():
                sum_copy(s).start()

        j = s - lag

        @pl.when((j >= 0) & (j < chunks))
        def _():
            middle_copy(j).wait_recv()

            @pl.when(is_mid)
            def _():
                total = kept[lax.rem(j, 2)] + from_inner[j].astype(f32)
                value, slopes = gelu_parts(total[0])
                from_inner[j, 0] = value.astype(bf16)
                from_inner[j, 1] = (total[1] * slopes).astype(bf16)

            @pl.when(has_outer)
            def _():
                result_copy(j).start()

            cut = pl.ds(pl.multiple_of(j * CHUNK, CHUNK), CHUNK)
            act[:, cut] = from_inner[j, 0]
            hg[:, cut] = from_inner[j, 1]
            out_acc[...] += jnp.dot(from_inner[j, 0], wout[j], preferred_element_type=f32)
            ig_acc[...] += contract_last(from_inner[j, 1], win[j])

    lax.fori_loop(0, chunks + 1 + 3 * (half - 1), step, None)

    for a in range(2):
        for k in range(1, chips):
            send_block(a, k).wait_send()
        for k in range(chips):
            share_block(a, k).wait_send()

    @pl.loop(0, chunks)
    def _(j):
        sum_copy(j).wait_send()

        @pl.when(has_outer)
        def _():
            result_copy(j).wait_send()


def layer(rows, cols, inputs, out_grad, w_in, w_out):
    tokens, feats = inputs.shape
    units = w_in.shape[1]
    chunks, batch = units // CHUNK, rows * tokens
    vmem = pl.BlockSpec(memory_space=pltpu.VMEM)
    far = pl.BlockSpec(memory_space=pl.ANY)
    dma = pltpu.SemaphoreType.DMA
    piece = (chunks, 2, batch, CHUNK)
    return pl.pallas_call(
        functools.partial(layer_kernel, rows, cols),
        out_shape=(
            jax.ShapeDtypeStruct((batch, feats), bf16),
            jax.ShapeDtypeStruct((batch, feats), bf16),
            jax.ShapeDtypeStruct((batch, units), bf16),
            jax.ShapeDtypeStruct((batch, units), bf16),
            jax.ShapeDtypeStruct((batch, feats), f32),
            jax.ShapeDtypeStruct((batch, feats), f32),
        ),
        in_specs=[vmem, vmem, far, far],
        out_specs=[vmem] * 6,
        scratch_shapes=[
            pltpu.VMEM((2, rows, tokens, feats), bf16),
            pltpu.VMEM((chunks, feats, CHUNK), bf16),
            pltpu.VMEM((chunks, CHUNK, feats), bf16),
            pltpu.VMEM(piece, bf16),
            pltpu.VMEM(piece, bf16),
            pltpu.VMEM(piece, bf16),
            pltpu.VMEM((2, 2, batch, CHUNK), f32),
            dma((2, rows // 2)),
            dma((2, rows)),
            dma((2, rows // 2)),
            dma((2, chunks)),
            dma((chunks,)),
            dma((chunks,)),
            dma((chunks,)),
            dma((chunks,)),
        ],
        compiler_params=pltpu.CompilerParams(
            collective_id=0, has_side_effects=True, vmem_limit_bytes=64 * 1024 * 1024 - 65536
        ),
        cost_estimate=pl.CostEstimate(
            flops=8 * batch * feats * units, bytes_accessed=4 * feats * units, transcendentals=0
        ),
    )(inputs, out_grad, w_in, w_out)


def grad_kernel(left, right, out):
    out[...] = contract_first(left[...], right[...]).astype(bf16)


def weight_grad(left, right):
    batch, height = left.shape
    width = right.shape[1]
    return pl.pallas_call(
        grad_kernel,
        grid=(height // CHUNK,),
        out_shape=jax.ShapeDtypeStruct((height, width), bf16),
        in_specs=[
            pl.BlockSpec((batch, CHUNK), lambda i: (0, i)),
            pl.BlockSpec((batch, width), lambda i: (0, 0)),
        ],
        out_specs=pl.BlockSpec((CHUNK, width), lambda i: (i, 0)),
        compiler_params=pltpu.CompilerParams(vmem_limit_bytes=32 * 1024 * 1024),
        cost_estimate=pl.CostEstimate(
            flops=2 * batch * height * width, bytes_accessed=2 * height * width, transcendentals=0
        ),
    )(left, right)


def local(rows, cols, inputs, w_in, w_out, out_grad):
    tokens, feats = inputs.shape
    chips = rows // 2
    x, og, act, hg, out_part, ig_part = layer(rows, cols, inputs, out_grad, w_in, w_out)
    row = lax.axis_index("row")
    chip, core = row // 2, row % 2

    parts = jnp.stack((out_part, ig_part)).reshape(2, chips, 2, tokens, feats)
    mine = lax.dynamic_index_in_dim(parts, core, 2, keepdims=False)
    theirs = lax.dynamic_index_in_dim(parts, 1 - core, 2, keepdims=False)
    pairs = [(r, r ^ 1) for r in range(rows)]
    summed = mine + lax.ppermute(theirs, "row", pairs)
    total = lax.dynamic_index_in_dim(summed, chip, 1, keepdims=False)
    for k in range(1, chips):
        block = lax.dynamic_index_in_dim(summed, (chip + k) % chips, 1, keepdims=False)
        shift = [(r, (r + 2 * k) % rows) for r in range(rows)]
        total = total + lax.ppermute(block.astype(bf16), "row", shift).astype(f32)
    total = total.astype(bf16)

    grad_out_w = weight_grad(act, og)
    grad_in_w = weight_grad(x, hg)
    return (total[0], total[1], grad_in_w, grad_out_w)


def solution(mesh):
    placed = (P("row", "col"), P("col", "row"), P("row", "col"), P("row", "col"))
    return jax.shard_map(
        functools.partial(local, mesh.shape["row"], mesh.shape["col"]),
        mesh=mesh,
        in_specs=placed,
        out_specs=(P("row", "col"), P("row", "col"), P("col", "row"), P("row", "col")),
        check_vma=False,
    )
```

time: 359 us -> 132 us (0.37)
  waiting for transfers between devices: 240 us -> 1.07 us
  Pallas kernels: 0 us -> 116 us
  matrix products: 71.4 us -> 0 us
  local copies, waits for them, and re-layouts: 26.2 us -> 3.33 us
  between operations: 13.8 us -> 0.7 us
    psum x1 -> x0, waiting for transfers between devices: 172 us -> none  [local(): hidden = lax.psum(hidden_part, 'col')]
    pallas_call x0 -> x3, Pallas kernels: none -> 116 us  [the longest x1 93.8 us: layer(): pl.pallas_call(functools.partial(layer_kernel, rows, cols), out_shape=(ja...]
    dot_general x6 -> x0, matrix products: 71.4 us -> none  [the longest x2 26.5 us: contract_last(): lax.dot_general(left, right, (((1,), (1,)), ((), ())), preferred_element_...]
    all_gather x2 -> x0, waiting for transfers between devices: 42 us -> none  [the longest x1 28 us: local(): lax.all_gather(inputs, 'row', axis=0, tiled=True)]
    unnamed x5 -> x10, local copies, waits for them, and re-layouts: 26.2 us -> 0.83 us
    reduce_scatter x2 -> x0, waiting for transfers between devices: 24.2 us -> none  [the longest x1 24.2 us: local(): lax.psum_scatter(contract_last(picked, w_in), 'row', scatter_dimension=0,...]
    convert_element_type x3 -> x1, other arithmetic: 6.42 us -> 0.13 us  [local(): total = total.astype(bf16)]
    another operation x0 -> x1, other arithmetic: none -> 4.29 us  [local(): parts = jnp.stack((out_part, ig_part)).reshape(2, chips, 2, tokens, feats)]
  transfers between devices with their start and end apart: 5 -> 4, of which waited for: 4 -> 2; matrix products, arithmetic and copies ran while one was open for 21% -> 0% of each run, Pallas kernels for 0% -> 17%
where the time goes in v1:
time: 132 us; the launch traced here: 131 us
  Pallas kernels  116 us (88%)
  other arithmetic  6.5 us (5%)
  starting transfers between devices  3.66 us (3%)
  local copies, waits for them, and re-layouts  3.33 us (3%)
    pallas_call x1, Pallas kernels, layer(): pl.pallas_call(functools.partial(layer_kernel, rows, cols), out_shape=(ja...  93.8 us
    pallas_call x2, Pallas kernels, weight_grad(): pl.pallas_call(grad_kernel, grid=(height // CHUNK,), out_shape=jax.ShapeD...  22.3 us
    another operation x1, other arithmetic, local(): parts = jnp.stack((out_part, ig_part)).reshape(2, chips, 2, tokens, feats)  4.29 us
    ppermute x3, starting transfers between devices, local(): total = total + lax.ppermute(block.astype(bf16), 'row', shift).astype(f32)  3.66 us
  transfers between devices with their start and end apart: 4, of which 2 were waited for; matrix products, arithmetic and copies ran while one was open for 0% of the time, Pallas kernels for 17%

profile of v1, /device:TPU:0, one launch (start us, length us, event | category | flops | bytes accessed | tf_op | source)
XLA Modules:
  0.0 131.4 jit_solution(16165239907842934954)
XLA Ops:
  0.7 93.8 %shard_map.75 = (bf16[192,3072]{1,0:T(8,128)(2,1)}, bf16[192,3072]{1,0:T(8,128)(2,1)}, bf16[192,3072]{1,0:T(8,128)(2,1)}, bf16[192,3072]{1,0:T(8,128)(2,1)}, f32[192,3072]{1,0:T(8,128)}, /*index=5*/f32[192,3072]{1,0:T(8,128)}) custom-call(bf16[24,3072]{1,0:T(8,128)(2,1)} %own_in.1, bf16[24,3072]{1,0:T(8,128)(2,1)} %own_grad.1, bf16[3072,3072]{1,0:T(8,128)(2,1)} %w_in.1, ...), custom_call_target="tpu_custom_call" | custom-call | flops 14495514624 | bytes 37748736 | tf_op jit(solution)/shard_map/pallas_call | solution.py:223
  94.5 4.3 %fusion.1 = (f32[2,4,1,24,3072]{4,3,2,1,0:T(8,128)}, f32[2,4,1,24,3072]{4,3,2,1,0:T(8,128)S(1)}) fusion(s32[]{:T(128)S(6)} %select_n.44, f32[1,4,2,24,3072]{4,3,2,1,0:T(8,128)} %bitcast.25, f32[1,4,2,24,3072]{4,3,2,1,0:T(8,128)} %bitcast.26, s32[]{:T(128)S(6)} %select_n.45), kind=kLoop, calls=%fused_computation.5 | loop fusion | flops 1179648 | bytes 9437192 | tf_op jit(solution)/shard_map/stack | solution.py:291
  98.8 0.0 copy-start.2
  98.8 0.0 copy-start.3
  98.8 1.7 %copy.12 = f32[2,4,1,24,3072]{4,3,0,1,2:T(8,128)} copy(f32[2,4,1,24,3072]{4,3,2,1,0:T(8,128)S(1)} %get-tuple-element.17) | data formatting | bytes 4718592 | tf_op jit(solution)/shard_map/jit(dynamic_index_in_dim)/dynamic_slice | solution.py:293
  100.4 0.0 collective-permute-start
  100.4 0.0 copy-done.2
  100.4 0.8 copy-done.3
  101.2 0.0 copy-start.4
  101.2 11.1 %shard_map.76 = bf16[3072,3072]{1,0:T(8,128)(2,1)} custom-call(bf16[192,3072]{1,0:T(8,128)(2,1)S(1)} %copy-done.2, bf16[192,3072]{1,0:T(8,128)(2,1)S(1)} %copy-done.3), custom_call_target="tpu_custom_call" | custom-call | flops 3623878656 | bytes 18874368 | tf_op jit(solution)/shard_map/pallas_call | solution.py:268
  112.4 0.0 collective-permute-done
  112.4 0.0 copy-done.4
  112.4 0.0 copy-start.1
  112.4 2.1 %bitcast_add_fusion = f32[2,4,24,3072]{3,2,0,1:T(8,128)S(1)} fusion(f32[2,4,24,3072]{3,2,0,1:T(8,128)} %collective-permute-done, f32[2,4,1,24,3072]{4,3,2,1,0:T(8,128)S(1)} %copy-done.4), kind=kLoop, calls=%fused_computation.6 | loop fusion | flops 589824 | bytes 7077888 | tf_op jit(solution)/shard_map/add | solution.py:295
  114.5 0.0 copy-start
  114.5 0.1 fusion.5
  114.6 1.1 collective-permute-start.1
  115.7 1.9 %collective-permute-start.3 = (bf16[2,24,3072]{2,1,0:T(8,128)(2,1)S(1)}, bf16[2,24,3072]{2,1,0:T(8,128)(2,1)S(1)}, u32[]{:S(2)}, u32[]{:S(2)}) collective-permute-start(bf16[2,24,3072]{2,1,0:T(8,128)(2,1)S(1)} %get-tuple-element.19), channel_id=1, source_target_pairs={{0,24},{4,28},{8,0},{12,4},{16,8},{20,12},{24,16},{28,20},{1,25},{... | collective-permute-start | bytes 884744 | tf_op jit(solution)/shard_map/ppermute | solution.py:300
  117.6 0.7 collective-permute-start.2
  118.3 0.0 copy-done.1
  118.3 0.0 copy-done
  118.3 11.1 %shard_map.77 = bf16[3072,3072]{1,0:T(8,128)(2,1)} custom-call(bf16[192,3072]{1,0:T(8,128)(2,1)S(1)} %copy-done.1, bf16[192,3072]{1,0:T(8,128)(2,1)S(1)} %copy-done), custom_call_target="tpu_custom_call" | custom-call | flops 3623878656 | bytes 18874368 | tf_op jit(solution)/shard_map/pallas_call | solution.py:268
  129.4 0.0 collective-permute-done.1
  129.4 0.3 collective-permute-done.3
  129.8 0.7 collective-permute-done.2
  130.5 0.1 fusion.4
  130.6 0.7 slice_bitcast_fusion
Async XLA Ops:
  98.8 1.7 %copy-start.2 = (bf16[192,3072]{1,0:T(8,128)(2,1)S(1)}, bf16[192,3072]{1,0:T(8,128)(2,1)}, u32[]{:S(2)}) copy-start(bf16[192,3072]{1,0:T(8,128)(2,1)} %get-tuple-element.12.left) | copy-start | bytes 3538948
  98.8 2.5 %copy-start.3 = (bf16[192,3072]{1,0:T(8,128)(2,1)S(1)}, bf16[192,3072]{1,0:T(8,128)(2,1)}, u32[]{:S(2)}) copy-start(bf16[192,3072]{1,0:T(8,128)(2,1)} %get-tuple-element.13.right) | copy-start | bytes 3538948
  100.4 12.0 %collective-permute-start = (f32[2,4,24,3072]{3,2,0,1:T(8,128)}, f32[2,4,24,3072]{3,2,0,1:T(8,128)}, u32[]{:S(2)}, u32[]{:S(2)}) collective-permute-start(f32[2,4,24,3072]{3,2,0,1:T(8,128)} %bitcast.24), channel_id=1, source_target_pairs={{0,4},{4,0},{8,12},{12,8},{16,20},{20,16},{24,28},{28,24},{1,5},{5... | collective-permute-start | bytes 7077896 | tf_op jit(solution)/shard_map/ppermute | solution.py:295
  101.2 11.2 %copy-start.4 = (f32[2,4,1,24,3072]{4,3,2,1,0:T(8,128)S(1)}, f32[2,4,1,24,3072]{4,3,2,1,0:T(8,128)}, u32[]{:S(2)}) copy-start(f32[2,4,1,24,3072]{4,3,2,1,0:T(8,128)} %get-tuple-element.16) | copy-start | bytes 7077892
  112.4 5.9 %copy-start.1 = (bf16[192,3072]{1,0:T(8,128)(2,1)S(1)}, bf16[192,3072]{1,0:T(8,128)(2,1)}, u32[]{:S(2)}) copy-start(bf16[192,3072]{1,0:T(8,128)(2,1)} %get-tuple-element.14.left) | copy-start | bytes 3538948
  114.5 3.8 %copy-start = (bf16[192,3072]{1,0:T(8,128)(2,1)S(1)}, bf16[192,3072]{1,0:T(8,128)(2,1)}, u32[]{:S(2)}) copy-start(bf16[192,3072]{1,0:T(8,128)(2,1)} %get-tuple-element.15.right) | copy-start | bytes 3538948
  114.6 14.8 %collective-permute-start.1 = (bf16[2,24,3072]{2,1,0:T(8,128)(2,1)S(1)}, bf16[2,24,3072]{2,1,0:T(8,128)(2,1)S(1)}, u32[]{:S(2)}, u32[]{:S(2)}) collective-permute-start(bf16[2,24,3072]{2,1,0:T(8,128)(2,1)S(1)} %get-tuple-element.18), channel_id=1, source_target_pairs={{0,8},{4,12},{8,16},{12,20},{16,24},{20,28},{24,0},{28,4},{1,9},{5... | collective-permute-start | bytes 884744 | tf_op jit(solution)/shard_map/ppermute | solution.py:300
  115.7 14.1 %collective-permute-start.3 = (bf16[2,24,3072]{2,1,0:T(8,128)(2,1)S(1)}, bf16[2,24,3072]{2,1,0:T(8,128)(2,1)S(1)}, u32[]{:S(2)}, u32[]{:S(2)}) collective-permute-start(bf16[2,24,3072]{2,1,0:T(8,128)(2,1)S(1)} %get-tuple-element.19), channel_id=1, source_target_pairs={{0,24},{4,28},{8,0},{12,4},{16,8},{20,12},{24,16},{28,20},{1,25},{... | collective-permute-start | bytes 884744 | tf_op jit(solution)/shard_map/ppermute | solution.py:300
  117.6 12.9 %collective-permute-start.2 = (bf16[2,24,3072]{2,1,0:T(8,128)(2,1)S(1)}, bf16[2,24,3072]{2,1,0:T(8,128)(2,1)S(1)}, u32[]{:S(2)}, u32[]{:S(2)}) collective-permute-start(bf16[2,24,3072]{2,1,0:T(8,128)(2,1)S(1)} %get-tuple-element.20), channel_id=1, source_target_pairs={{0,16},{4,20},{8,24},{12,28},{16,0},{20,4},{24,8},{28,12},{1,17},{... | collective-permute-start | bytes 884744 | tf_op jit(solution)/shard_map/ppermute | solution.py:300

commit v2 on v1

--- a/solution.py
+++ b/solution.py
@@ -11,6 +11,7 @@
 gelu_cubic = 0.044715
 MESH = pl.DeviceIdType.MESH
 CHUNK = 256
+BLOCK = 768
 f32, bf16 = jnp.float32, jnp.bfloat16
 
 
@@ -33,11 +34,15 @@
 
 
 def layer_kernel(
-    rows, cols, own_in, own_grad, w_in, w_out,
-    x, og, act, hg, out_acc, ig_acc,
-    slab, win, wout, from_outer, from_inner, to_inner, kept,
-    gather_send, gather_recv, share_send, w_sem, outer_sem, inner_sem, in_send, out_send,
+    rows, cols, own_in, own_grad, w_in, w_out, *refs
 ):
+    (x_far, og_far, act, hg, own_sum), others = refs[:5], refs[5 : 4 + rows // 2]
+    (
+        x, og, out_acc, ig_acc, pair,
+        slab, win, wout, from_outer, from_inner, to_inner, kept, early,
+        gather_send, gather_recv, share_send, w_sem, outer_sem, inner_sem, in_send, out_send,
+        far_sem, act_sem, pair_send, pair_recv,
+    ) = refs[4 + rows // 2 :]
     row, col = lax.axis_index("row"), lax.axis_index("col")
     chips, half = rows // 2, cols // 2
     chip, core = row // 2, row % 2
@@ -102,10 +107,21 @@
             recv_sem=gather_recv.at[a, source], device_id=(sibling, col), device_id_type=MESH,
         ).wait_recv()
 
-    for a in range(2):
-        for k in range(1, chips):
-            send_block(a, k).start()
-        share_block(a, 0).start()
+    def far_copy(a):
+        return pltpu.make_async_copy((x, og)[a], (x_far, og_far)[a], far_sem.at[a])
+
+    def early_step(s, _):
+        weight_copies(s)[0].wait()
+        early[s] = jnp.dot(x[...], win[s], preferred_element_type=f32)
+
+    for k in range(1, chips):
+        send_block(0, k).start()
+    share_block(0, 0).start()
+    for k in range(1, chips):
+        send_block(0, k).wait_send()
+    for k in range(1, chips):
+        send_block(1, k).start()
+    share_block(1, 0).start()
     for a, (whole, wide) in enumerate(((x, out_acc), (og, ig_acc))):
         for k in range(1, chips):
             arrived(a, lax.rem(chip + chips - k, chips) * 2 + core)
@@ -127,6 +143,9 @@
         lax.fori_loop(0, rows, unfold, None)
         whole[...] = wide[...].astype(bf16)
         wide[...] = jnp.zeros_like(wide)
+        far_copy(a).start()
+        if a == 0:
+            lax.fori_loop(0, early.shape[0], early_step, None)
 
     def sum_copy(j):
         return pltpu.make_async_remote_copy(
@@ -144,6 +163,23 @@
         return pltpu.make_async_remote_copy(
             src_ref=from_inner.at[j], dst_ref=from_inner.at[j], send_sem=out_send.at[j],
             recv_sem=inner_sem.at[j], device_id=(row, outer), device_id_type=MESH,
+        )
+
+    def act_copies(j):
+        cut = pl.ds(pl.multiple_of(j * CHUNK, CHUNK), CHUNK)
+        return tuple(
+            pltpu.make_async_copy(from_inner.at[j, a], far.at[:, cut], act_sem.at[a, j])
+            for a, far in enumerate((act, hg))
+        )
+
+    def token_rows(q, which):
+        return pl.ds(pl.multiple_of((q * 2 + which) * tokens, 8), tokens)
+
+    def pair_copy(a, q):
+        return pltpu.make_async_remote_copy(
+            src_ref=(out_acc, ig_acc)[a].at[token_rows(q, 1 - core), :], dst_ref=pair.at[a, q],
+            send_sem=pair_send.at[a, q], recv_sem=pair_recv.at[a, q],
+            device_id=(sibling, col), device_id_type=MESH,
         )
 
     lag = 1 + 3 * away
@@ -151,10 +187,18 @@
     def step(s, _):
         @pl.when(s < chunks)
         def _():
-            for copy in weight_copies(s):
-                copy.wait()
+            weight_copies(s)[1].wait()
             slot = lax.rem(s, 2)
-            kept[slot, 0] = jnp.dot(x[...], win[s], preferred_element_type=f32)
+
+            @pl.when(s < early.shape[0])
+            def _():
+                kept[slot, 0] = early[s]
+
+            @pl.when(s >= early.shape[0])
+            def _():
+                weight_copies(s)[0].wait()
+                kept[slot, 0] = jnp.dot(x[...], win[s], preferred_element_type=f32)
+
             kept[slot, 1] = contract_last(og[...], wout[s])
 
             @pl.when(has_outer)
@@ -189,23 +233,47 @@
             def _():
                 result_copy(j).start()
 
-            cut = pl.ds(pl.multiple_of(j * CHUNK, CHUNK), CHUNK)
-            act[:, cut] = from_inner[j, 0]
-            hg[:, cut] = from_inner[j, 1]
+            for copy in act_copies(j):
+                copy.start()
             out_acc[...] += jnp.dot(from_inner[j, 0], wout[j], preferred_element_type=f32)
+
+            @pl.when(j == chunks - 1)
+            def _():
+                for q in range(chips):
+                    pair_copy(0, q).start()
+
             ig_acc[...] += contract_last(from_inner[j, 1], win[j])
 
     lax.fori_loop(0, chunks + 1 + 3 * (half - 1), step, None)
 
+    for q in range(chips):
+        pair_copy(1, q).start()
+    for a, acc in enumerate((out_acc, ig_acc)):
+        for q in range(chips):
+            pair_copy(a, q).wait_recv()
+        for k in range(chips):
+            q = lax.rem(chip + k, chips)
+            block = acc[token_rows(q, core), :] + pair[a, q]
+            if k == 0:
+                own_sum[a] = block
+            else:
+                others[k - 1][a] = block.astype(bf16)
+        for q in range(chips):
+            pair_copy(a, q).wait_send()
+
     for a in range(2):
-        for k in range(1, chips):
-            send_block(a, k).wait_send()
+        far_copy(a).wait()
+        if a == 1:
+            for k in range(1, chips):
+                send_block(a, k).wait_send()
         for k in range(chips):
             share_block(a, k).wait_send()
 
     @pl.loop(0, chunks)
     def _(j):
         sum_copy(j).wait_send()
+        for copy in act_copies(j):
+            copy.wait()
 
         @pl.when(has_outer)
         def _():
@@ -227,12 +295,17 @@
             jax.ShapeDtypeStruct((batch, feats), bf16),
             jax.ShapeDtypeStruct((batch, units), bf16),
             jax.ShapeDtypeStruct((batch, units), bf16),
-            jax.ShapeDtypeStruct((batch, feats), f32),
-            jax.ShapeDtypeStruct((batch, feats), f32),
-        ),
+            jax.ShapeDtypeStruct((2, tokens, feats), f32),
+        )
+        + (jax.ShapeDtypeStruct((2, tokens, feats), bf16),) * (rows // 2 - 1),
         in_specs=[vmem, vmem, far, far],
-        out_specs=[vmem] * 6,
+        out_specs=[far] * 4 + [vmem] * (rows // 2),
         scratch_shapes=[
+            pltpu.VMEM((batch, feats), bf16),
+            pltpu.VMEM((batch, feats), bf16),
+            pltpu.VMEM((batch, feats), f32),
+            pltpu.VMEM((batch, feats), f32),
+            pltpu.VMEM((2, rows // 2, tokens, feats), f32),
             pltpu.VMEM((2, rows, tokens, feats), bf16),
             pltpu.VMEM((chunks, feats, CHUNK), bf16),
             pltpu.VMEM((chunks, CHUNK, feats), bf16),
@@ -240,6 +313,7 @@
             pltpu.VMEM(piece, bf16),
             pltpu.VMEM(piece, bf16),
             pltpu.VMEM((2, 2, batch, CHUNK), f32),
+            pltpu.VMEM(((chunks + 1) // 2, batch, CHUNK), f32),
             dma((2, rows // 2)),
             dma((2, rows)),
             dma((2, rows // 2)),
@@ -248,6 +322,10 @@
             dma((chunks,)),
             dma((chunks,)),
             dma((chunks,)),
+            dma((2,)),
+            dma((2, chunks)),
+            dma((2, rows // 2)),
+            dma((2, rows // 2)),
         ],
         compiler_params=pltpu.CompilerParams(
             collective_id=0, has_side_effects=True, vmem_limit_bytes=64 * 1024 * 1024 - 65536
@@ -258,23 +336,43 @@
     )(inputs, out_grad, w_in, w_out)
 
 
-def grad_kernel(left, right, out):
+def grad_rows_kernel(left, right, out):
     out[...] = contract_first(left[...], right[...]).astype(bf16)
 
 
-def weight_grad(left, right):
+def grad_columns_kernel(left, right, out, turned):
+    @pl.when(pl.program_id(0) == 0)
+    def _():
+        turned[...] = left[...].T
+
+    out[...] = jnp.dot(turned[...], right[...], preferred_element_type=f32).astype(bf16)
+
+
+def weight_grad(left, right, by_rows):
     batch, height = left.shape
     width = right.shape[1]
+    if by_rows:
+        grid, body, scratch = height // BLOCK, grad_rows_kernel, []
+        in_specs = [
+            pl.BlockSpec((batch, BLOCK), lambda i: (0, i)),
+            pl.BlockSpec((batch, width), lambda i: (0, 0)),
+        ]
+        out_specs = pl.BlockSpec((BLOCK, width), lambda i: (i, 0))
+    else:
+        grid, body, scratch = width // CHUNK, grad_columns_kernel, [pltpu.VMEM((height, batch), bf16)]
+        in_specs = [
+            pl.BlockSpec((batch, height), lambda i: (0, 0)),
+            pl.BlockSpec((batch, CHUNK), lambda i: (0, i)),
+        ]
+        out_specs = pl.BlockSpec((height, CHUNK), lambda i: (0, i))
     return pl.pallas_call(
-        grad_kernel,
-        grid=(height // CHUNK,),
+        body,
+        grid=(grid,),
         out_shape=jax.ShapeDtypeStruct((height, width), bf16),
-        in_specs=[
-            pl.BlockSpec((batch, CHUNK), lambda i: (0, i)),
-            pl.BlockSpec((batch, width), lambda i: (0, 0)),
-        ],
-        out_specs=pl.BlockSpec((CHUNK, width), lambda i: (i, 0)),
-        compiler_params=pltpu.CompilerParams(vmem_limit_bytes=32 * 1024 * 1024),
+        in_specs=in_specs,
+        out_specs=out_specs,
+        scratch_shapes=scratch,
+        compiler_params=pltpu.CompilerParams(vmem_limit_bytes=48 * 1024 * 1024),
         cost_estimate=pl.CostEstimate(
             flops=2 * batch * height * width, bytes_accessed=2 * height * width, transcendentals=0
         ),
@@ -284,24 +382,15 @@
 def local(rows, cols, inputs, w_in, w_out, out_grad):
     tokens, feats = inputs.shape
     chips = rows // 2
-    x, og, act, hg, out_part, ig_part = layer(rows, cols, inputs, out_grad, w_in, w_out)
-    row = lax.axis_index("row")
-    chip, core = row // 2, row % 2
-
-    parts = jnp.stack((out_part, ig_part)).reshape(2, chips, 2, tokens, feats)
-    mine = lax.dynamic_index_in_dim(parts, core, 2, keepdims=False)
-    theirs = lax.dynamic_index_in_dim(parts, 1 - core, 2, keepdims=False)
-    pairs = [(r, r ^ 1) for r in range(rows)]
-    summed = mine + lax.ppermute(theirs, "row", pairs)
-    total = lax.dynamic_index_in_dim(summed, chip, 1, keepdims=False)
+    x, og, act, hg, total, *blocks = layer(rows, cols, inputs, out_grad, w_in, w_out)
+
     for k in range(1, chips):
-        block = lax.dynamic_index_in_dim(summed, (chip + k) % chips, 1, keepdims=False)
         shift = [(r, (r + 2 * k) % rows) for r in range(rows)]
-        total = total + lax.ppermute(block.astype(bf16), "row", shift).astype(f32)
+        total = total + lax.ppermute(blocks[k - 1], "row", shift).astype(f32)
     total = total.astype(bf16)
 
-    grad_out_w = weight_grad(act, og)
-    grad_in_w = weight_grad(x, hg)
+    grad_out_w = weight_grad(act, og, True)
+    grad_in_w = weight_grad(x, hg, False)
     return (total[0], total[1], grad_in_w, grad_out_w)
 
 

time: 132 us -> 123 us (0.932)
  other arithmetic: 6.5 us -> 0.13 us
    another operation x1 -> x0, other arithmetic: 4.29 us -> none  [local(): parts = jnp.stack((out_part, ig_part)).reshape(2, chips, 2, tokens, feats)]
    add x1 -> x0, other arithmetic: 2.08 us -> none  [local(): summed = mine + lax.ppermute(theirs, 'row', pairs)]
    pallas_call x2, Pallas kernels: 22.3 us -> 20.3 us  [weight_grad(): pl.pallas_call(body, grid=(grid,), out_shape=jax.ShapeDtypeStruct((height...]
    unnamed x10, local copies, waits for them, and re-layouts: 0.83 us -> 2.55 us
    dynamic_slice x1 -> x0, local copies, waits for them, and re-layouts: 1.66 us -> none  [local(): theirs = lax.dynamic_index_in_dim(parts, 1 - core, 2, keepdims=False)]
    pallas_call x1, Pallas kernels: 93.8 us -> 95.2 us  [layer(): pl.pallas_call(functools.partial(layer_kernel, rows, cols), out_shape=(ja...]
    ppermute x4 -> x3, starting transfers between devices: 3.66 us -> 3.7 us  [local(): total = total + lax.ppermute(blocks[k - 1], 'row', shift).astype(f32)]
  transfers between devices with their start and end apart: 4 -> 3, of which waited for: 2 -> 0; matrix products, arithmetic and copies ran while one was open for 0% -> 0% of each run, Pallas kernels for 17% -> 16%
where the time goes in v2:
time: 123 us
  Pallas kernels  115 us (93%)
  starting transfers between devices  3.7 us (3%)
  local copies, waits for them, and re-layouts  3.28 us (3%)
    pallas_call x1, Pallas kernels, layer(): pl.pallas_call(functools.partial(layer_kernel, rows, cols), out_shape=(ja...  95.2 us
    pallas_call x2, Pallas kernels, weight_grad(): pl.pallas_call(body, grid=(grid,), out_shape=jax.ShapeDtypeStruct((height...  20.3 us
    ppermute x3, starting transfers between devices, local(): total = total + lax.ppermute(blocks[k - 1], 'row', shift).astype(f32)  3.7 us
    unnamed x10, local copies, waits for them, and re-layouts  2.55 us
  transfers between devices with their start and end apart: 3, of which 0 were waited for; matrix products, arithmetic and copies ran while one was open for 0% of the time, Pallas kernels for 16%

profile of v2, /device:TPU:0, one launch (start us, length us, event | category | flops | bytes accessed | tf_op | source)
XLA Modules:
  0.0 123.3 jit_solution(11493485583875460563)
XLA Ops:
  0.6 95.2 %shard_map.75 = (bf16[192,3072]{1,0:T(8,128)(2,1)}, bf16[192,3072]{1,0:T(8,128)(2,1)}, bf16[192,3072]{1,0:T(8,128)(2,1)}, bf16[192,3072]{1,0:T(8,128)(2,1)}, f32...) custom-call(bf16[24,3072]{1,0:T(8,128)(2,1)} %own_in.1, ...), custom_call_target="tpu_custom_call" | custom-call | flops 14495514624 | bytes 37748736 | tf_op jit(solution)/shard_map/pallas_call | solution.py:291
  95.9 0.0 copy-start
  95.9 0.0 copy-start.1
  95.9 0.9 collective-permute-start
  96.7 1.7 %collective-permute-start.1 = (bf16[2,24,3072]{2,1,0:T(8,128)(2,1)}, bf16[2,24,3072]{2,1,0:T(8,128)(2,1)S(1)}, u32[]{:S(2)}, u32[]{:S(2)}) collective-permute-start(bf16[2,24,3072]{2,1,0:T(8,128)(2,1)} %get-tuple-element.14), channel_id=1, source_target_pairs={{0,16},{4,20},{8,24},{12,28},{16,0},{20,4},{24,8},{28,12},{1,17},{... | collective-permute-start | bytes 884744 | tf_op jit(solution)/shard_map/ppermute | solution.py:389
  98.4 1.1 collective-permute-start.2
  99.6 0.0 copy-start.2
  99.6 1.3 %copy-done.2 = bf16[192,3072]{1,0:T(8,128)(2,1)S(1)} copy-done((bf16[192,3072]{1,0:T(8,128)(2,1)S(1)}, bf16[192,3072]{1,0:T(8,128)(2,1)}, u32[]{:S(2)}) %copy-start.2) | copy-done | bytes 1179672
  100.8 0.0 copy-start.3
  100.9 1.3 %copy-done.3 = bf16[192,3072]{1,0:T(8,128)(2,1)S(1)} copy-done((bf16[192,3072]{1,0:T(8,128)(2,1)S(1)}, bf16[192,3072]{1,0:T(8,128)(2,1)}, u32[]{:S(2)}) %copy-start.3) | copy-done | bytes 1179672
  102.1 0.0 copy-start.4
  102.1 11.4 %shard_map.76 = bf16[3072,3072]{1,0:T(8,128)(2,1)} custom-call(bf16[192,3072]{1,0:T(8,128)(2,1)S(1)} %copy-done.2, bf16[192,3072]{1,0:T(8,128)(2,1)S(1)} %copy-done.3), custom_call_target="tpu_custom_call" | custom-call | flops 3623878656 | bytes 18874368 | tf_op jit(solution)/shard_map/pallas_call | solution.py:368
  113.5 0.0 copy-done
  113.6 0.0 copy-done.1
  113.6 8.8 %shard_map.77 = bf16[3072,3072]{1,0:T(8,128)(2,1)} custom-call(bf16[192,3072]{1,0:T(8,128)(2,1)S(1)} %copy-done.1, bf16[192,3072]{1,0:T(8,128)(2,1)S(1)} %copy-done), custom_call_target="tpu_custom_call" | custom-call | flops 3623878656 | bytes 18874368 | tf_op jit(solution)/shard_map/pallas_call | solution.py:368
  122.4 0.0 collective-permute-done
  122.4 0.0 collective-permute-done.1
  122.4 0.0 collective-permute-done.2
  122.4 0.0 copy-done.4
  122.4 0.1 add_convert_fusion
  122.6 0.7 slice_bitcast_fusion
Async XLA Ops:
  95.9 17.7 %copy-start = (bf16[192,3072]{1,0:T(8,128)(2,1)S(1)}, bf16[192,3072]{1,0:T(8,128)(2,1)}, u32[]{:S(2)}) copy-start(bf16[192,3072]{1,0:T(8,128)(2,1)} %get-tuple-element.19.right) | copy-start | bytes 3538948
  95.9 17.7 %copy-start.1 = (bf16[192,3072]{1,0:T(8,128)(2,1)S(1)}, bf16[192,3072]{1,0:T(8,128)(2,1)}, u32[]{:S(2)}) copy-start(bf16[192,3072]{1,0:T(8,128)(2,1)} %get-tuple-element.18.left) | copy-start | bytes 3538948
  95.9 26.5 %collective-permute-start = (bf16[2,24,3072]{2,1,0:T(8,128)(2,1)}, bf16[2,24,3072]{2,1,0:T(8,128)(2,1)S(1)}, u32[]{:S(2)}, u32[]{:S(2)}) collective-permute-start(bf16[2,24,3072]{2,1,0:T(8,128)(2,1)} %get-tuple-element.13), channel_id=1, source_target_pairs={{0,8},{4,12},{8,16},{12,20},{16,24},{20,28},{24,0},{28,4},{1,9},{5... | collective-permute-start | bytes 884744 | tf_op jit(solution)/shard_map/ppermute | solution.py:389
  96.7 25.7 %collective-permute-start.1 = (bf16[2,24,3072]{2,1,0:T(8,128)(2,1)}, bf16[2,24,3072]{2,1,0:T(8,128)(2,1)S(1)}, u32[]{:S(2)}, u32[]{:S(2)}) collective-permute-start(bf16[2,24,3072]{2,1,0:T(8,128)(2,1)} %get-tuple-element.14), channel_id=1, source_target_pairs={{0,16},{4,20},{8,24},{12,28},{16,0},{20,4},{24,8},{28,12},{1,17},{... | collective-permute-start | bytes 884744 | tf_op jit(solution)/shard_map/ppermute | solution.py:389
  98.4 24.0 %collective-permute-start.2 = (bf16[2,24,3072]{2,1,0:T(8,128)(2,1)}, bf16[2,24,3072]{2,1,0:T(8,128)(2,1)S(1)}, u32[]{:S(2)}, u32[]{:S(2)}) collective-permute-start(bf16[2,24,3072]{2,1,0:T(8,128)(2,1)} %get-tuple-element.15), channel_id=1, source_target_pairs={{0,24},{4,28},{8,0},{12,4},{16,8},{20,12},{24,16},{28,20},{1,25},{... | collective-permute-start | bytes 884744 | tf_op jit(solution)/shard_map/ppermute | solution.py:389
  99.6 1.3 %copy-start.2 = (bf16[192,3072]{1,0:T(8,128)(2,1)S(1)}, bf16[192,3072]{1,0:T(8,128)(2,1)}, u32[]{:S(2)}) copy-start(bf16[192,3072]{1,0:T(8,128)(2,1)} %get-tuple-element.16.left) | copy-start | bytes 3538948
  100.8 1.3 %copy-start.3 = (bf16[192,3072]{1,0:T(8,128)(2,1)S(1)}, bf16[192,3072]{1,0:T(8,128)(2,1)}, u32[]{:S(2)}) copy-start(bf16[192,3072]{1,0:T(8,128)(2,1)} %get-tuple-element.17.right) | copy-start | bytes 3538948
  102.1 20.3 %copy-start.4 = (f32[2,24,3072]{2,1,0:T(8,128)S(1)}, f32[2,24,3072]{2,1,0:T(8,128)}, u32[]{:S(2)}) copy-start(f32[2,24,3072]{2,1,0:T(8,128)} %get-tuple-element.12) | copy-start | bytes 1769476

commit v3 on v2

--- a/solution.py
+++ b/solution.py
@@ -11,7 +11,7 @@
 gelu_cubic = 0.044715
 MESH = pl.DeviceIdType.MESH
 CHUNK = 256
-BLOCK = 768
+VMEM_BYTES = 64 * 1024 * 1024 - 65536
 f32, bf16 = jnp.float32, jnp.bfloat16
 
 
@@ -47,7 +47,9 @@
     chips, half = rows // 2, cols // 2
     chip, core = row // 2, row % 2
     sibling = chip * 2 + (1 - core)
-    chunks, tokens = win.shape[0], own_in.shape[0]
+    chunks, tokens = from_inner.shape[0], own_in.shape[0]
+    group = chunks // win.shape[0]
+    passed = early.shape[0] // 2
 
     lower = col < half
     inner = jnp.where(lower, col + 1, col - 1)
@@ -56,17 +58,16 @@
     is_mid = away == 0
     has_outer = away < half - 1
 
-    def weight_copies(j):
-        cut = pl.ds(pl.multiple_of(j * CHUNK, CHUNK), CHUNK)
-        return (
-            pltpu.make_async_copy(w_in.at[:, cut], win.at[j], w_sem.at[0, j]),
-            pltpu.make_async_copy(w_out.at[cut, :], wout.at[j], w_sem.at[1, j]),
-        )
-
-    @pl.loop(0, chunks)
-    def _(j):
-        for copy in weight_copies(j):
-            copy.start()
+    def units(j):
+        return pl.ds(pl.multiple_of(j * CHUNK, CHUNK), CHUNK)
+
+    def w_in_copy(j):
+        to = win.at[j // group, :, units(j % group)]
+        return pltpu.make_async_copy(w_in.at[:, units(j)], to, w_sem.at[0, j])
+
+    def w_out_copy(j):
+        to = wout.at[j // group, units(j % group), :]
+        return pltpu.make_async_copy(w_out.at[units(j), :], to, w_sem.at[1, j])
 
     barrier = pltpu.get_barrier_semaphore()
     for k in range(1, chips):
@@ -78,6 +79,14 @@
     @pl.when(has_outer)
     def _():
         pl.semaphore_signal(barrier, inc=1, device_id=(row, outer), device_id_type=MESH)
+
+    @pl.loop(0, chunks)
+    def _(j):
+        w_in_copy(j).start()
+        w_out_copy(j).start()
+
+    @pl.when(has_outer)
+    def _():
         pl.semaphore_wait(barrier, chips + 2)
 
     @pl.when(jnp.logical_not(has_outer))
@@ -110,9 +119,55 @@
     def far_copy(a):
         return pltpu.make_async_copy((x, og)[a], (x_far, og_far)[a], far_sem.at[a])
 
+    def sum_copy(a, j):
+        return pltpu.make_async_remote_copy(
+            src_ref=to_inner.at[j, a], dst_ref=from_outer.at[j, a], send_sem=in_send.at[a, j],
+            recv_sem=outer_sem.at[a, j], device_id=(row, inner), device_id_type=MESH,
+        )
+
+    def middle_copy(a, j):
+        return pltpu.make_async_remote_copy(
+            src_ref=to_inner.at[j, a], dst_ref=from_inner.at[j, a], send_sem=in_send.at[a, j],
+            recv_sem=inner_sem.at[a, j], device_id=(row, inner), device_id_type=MESH,
+        )
+
+    def result_copy(a, j):
+        return pltpu.make_async_remote_copy(
+            src_ref=from_inner.at[j, a], dst_ref=from_inner.at[j, a], send_sem=out_send.at[a, j],
+            recv_sem=inner_sem.at[a, j], device_id=(row, outer), device_id_type=MESH,
+        )
+
+    def pass_inward(a, j, part):
+        @pl.when(has_outer)
+        def _():
+            sum_copy(a, j).wait_recv()
+            part[...] = part[...] + from_outer[j, a].astype(f32)
+
+        to_inner[j, a] = part[...].astype(bf16)
+
+        @pl.when(is_mid)
+        def _():
+            middle_copy(a, j).start()
+
+        @pl.when(jnp.logical_not(is_mid))
+        def _():
+            sum_copy(a, j).start()
+
+    def hidden_part(s):
+        w_in_copy(s).wait()
+        return jnp.dot(x[...], win[s // group, :, units(s % group)], preferred_element_type=f32)
+
     def early_step(s, _):
-        weight_copies(s)[0].wait()
-        early[s] = jnp.dot(x[...], win[s], preferred_element_type=f32)
+        early[s] = hidden_part(s)
+
+        @pl.when(jnp.logical_not(has_outer))
+        def _():
+            pass_inward(0, s, early.at[s])
+
+    def early_pass(s, _):
+        @pl.when(has_outer)
+        def _():
+            pass_inward(0, s, early.at[s])
 
     for k in range(1, chips):
         send_block(0, k).start()
@@ -146,29 +201,11 @@
         far_copy(a).start()
         if a == 0:
             lax.fori_loop(0, early.shape[0], early_step, None)
-
-    def sum_copy(j):
-        return pltpu.make_async_remote_copy(
-            src_ref=to_inner.at[j], dst_ref=from_outer.at[j], send_sem=in_send.at[j],
-            recv_sem=outer_sem.at[j], device_id=(row, inner), device_id_type=MESH,
-        )
-
-    def middle_copy(j):
-        return pltpu.make_async_remote_copy(
-            src_ref=to_inner.at[j], dst_ref=from_inner.at[j], send_sem=in_send.at[j],
-            recv_sem=inner_sem.at[j], device_id=(row, inner), device_id_type=MESH,
-        )
-
-    def result_copy(j):
-        return pltpu.make_async_remote_copy(
-            src_ref=from_inner.at[j], dst_ref=from_inner.at[j], send_sem=out_send.at[j],
-            recv_sem=inner_sem.at[j], device_id=(row, outer), device_id_type=MESH,
-        )
+            lax.fori_loop(0, passed, early_pass, None)
 
     def act_copies(j):
-        cut = pl.ds(pl.multiple_of(j * CHUNK, CHUNK), CHUNK)
         return tuple(
-            pltpu.make_async_copy(from_inner.at[j, a], far.at[:, cut], act_sem.at[a, j])
+            pltpu.make_async_copy(from_inner.at[j, a], far.at[:, units(j)], act_sem.at[a, j])
             for a, far in enumerate((act, hg))
         )
 
@@ -187,40 +224,31 @@
     def step(s, _):
         @pl.when(s < chunks)
         def _():
-            weight_copies(s)[1].wait()
             slot = lax.rem(s, 2)
 
             @pl.when(s < early.shape[0])
             def _():
+                @pl.when(has_outer & (s >= passed))
+                def _():
+                    pass_inward(0, s, early.at[s])
+
                 kept[slot, 0] = early[s]
 
             @pl.when(s >= early.shape[0])
             def _():
-                weight_copies(s)[0].wait()
-                kept[slot, 0] = jnp.dot(x[...], win[s], preferred_element_type=f32)
-
-            kept[slot, 1] = contract_last(og[...], wout[s])
-
-            @pl.when(has_outer)
-            def _():
-                sum_copy(s).wait_recv()
-                kept[slot] = kept[slot] + from_outer[s].astype(f32)
-
-            to_inner[s] = kept[slot].astype(bf16)
-
-            @pl.when(is_mid)
-            def _():
-                middle_copy(s).start()
-
-            @pl.when(jnp.logical_not(is_mid))
-            def _():
-                sum_copy(s).start()
+                kept[slot, 0] = hidden_part(s)
+                pass_inward(0, s, kept.at[slot, 0])
+
+            w_out_copy(s).wait()
+            kept[slot, 1] = contract_last(og[...], wout[s // group, units(s % group), :])
+            pass_inward(1, s, kept.at[slot, 1])
 
         j = s - lag
 
         @pl.when((j >= 0) & (j < chunks))
         def _():
-            middle_copy(j).wait_recv()
+            middle_copy(0, j).wait_recv()
+            middle_copy(1, j).wait_recv()
 
             @pl.when(is_mid)
             def _():
@@ -231,18 +259,29 @@
 
             @pl.when(has_outer)
             def _():
-                result_copy(j).start()
+                result_copy(0, j).start()
+                result_copy(1, j).start()
 
             for copy in act_copies(j):
                 copy.start()
-            out_acc[...] += jnp.dot(from_inner[j, 0], wout[j], preferred_element_type=f32)
-
-            @pl.when(j == chunks - 1)
-            def _():
-                for q in range(chips):
-                    pair_copy(0, q).start()
-
-            ig_acc[...] += contract_last(from_inner[j, 1], win[j])
+
+            @pl.when(lax.rem(j, group) == group - 1)
+            def _():
+                g = j // group
+
+                def gathered(a):
+                    return jnp.concatenate(
+                        [from_inner[g * group + i, a] for i in range(group)], axis=1
+                    )
+
+                out_acc[...] += jnp.dot(gathered(0), wout[g], preferred_element_type=f32)
+
+                @pl.when(j == chunks - 1)
+                def _():
+                    for q in range(chips):
+                        pair_copy(0, q).start()
+
+                ig_acc[...] += contract_last(gathered(1), win[g])
 
     lax.fori_loop(0, chunks + 1 + 3 * (half - 1), step, None)
 
@@ -271,13 +310,15 @@
 
     @pl.loop(0, chunks)
     def _(j):
-        sum_copy(j).wait_send()
+        sum_copy(0, j).wait_send()
+        sum_copy(1, j).wait_send()
         for copy in act_copies(j):
             copy.wait()
 
         @pl.when(has_outer)
         def _():
-            result_copy(j).wait_send()
+            result_copy(0, j).wait_send()
+            result_copy(1, j).wait_send()
 
 
 def layer(rows, cols, inputs, out_grad, w_in, w_out):
@@ -287,6 +328,7 @@
     vmem = pl.BlockSpec(memory_space=pltpu.VMEM)
     far = pl.BlockSpec(memory_space=pl.ANY)
     dma = pltpu.SemaphoreType.DMA
+    group = 2 if chunks % 2 == 0 else 1
     piece = (chunks, 2, batch, CHUNK)
     return pl.pallas_call(
         functools.partial(layer_kernel, rows, cols),
@@ -307,8 +349,8 @@
             pltpu.VMEM((batch, feats), f32),
             pltpu.VMEM((2, rows // 2, tokens, feats), f32),
             pltpu.VMEM((2, rows, tokens, feats), bf16),
-            pltpu.VMEM((chunks, feats, CHUNK), bf16),
-            pltpu.VMEM((chunks, CHUNK, feats), bf16),
+            pltpu.VMEM((chunks // group, feats, group * CHUNK), bf16),
+            pltpu.VMEM((chunks // group, group * CHUNK, feats), bf16),
             pltpu.VMEM(piece, bf16),
             pltpu.VMEM(piece, bf16),
             pltpu.VMEM(piece, bf16),
@@ -318,17 +360,17 @@
             dma((2, rows)),
             dma((2, rows // 2)),
             dma((2, chunks)),
-            dma((chunks,)),
-            dma((chunks,)),
-            dma((chunks,)),
-            dma((chunks,)),
+            dma((2, chunks)),
+            dma((2, chunks)),
+            dma((2, chunks)),
+            dma((2, chunks)),
             dma((2,)),
             dma((2, chunks)),
             dma((2, rows // 2)),
             dma((2, rows // 2)),
         ],
         compiler_params=pltpu.CompilerParams(
-            collective_id=0, has_side_effects=True, vmem_limit_bytes=64 * 1024 * 1024 - 65536
+            collective_id=0, has_side_effects=True, vmem_limit_bytes=VMEM_BYTES
         ),
         cost_estimate=pl.CostEstimate(
             flops=8 * batch * feats * units, bytes_accessed=4 * feats * units, transcendentals=0
@@ -336,11 +378,7 @@
     )(inputs, out_grad, w_in, w_out)
 
 
-def grad_rows_kernel(left, right, out):
-    out[...] = contract_first(left[...], right[...]).astype(bf16)
-
-
-def grad_columns_kernel(left, right, out, turned):
+def grad_kernel(left, right, out, turned):
     @pl.when(pl.program_id(0) == 0)
     def _():
         turned[...] = left[...].T
@@ -348,31 +386,20 @@
     out[...] = jnp.dot(turned[...], right[...], preferred_element_type=f32).astype(bf16)
 
 
-def weight_grad(left, right, by_rows):
+def weight_grad(left, right):
     batch, height = left.shape
     width = right.shape[1]
-    if by_rows:
-        grid, body, scratch = height // BLOCK, grad_rows_kernel, []
-        in_specs = [
-            pl.BlockSpec((batch, BLOCK), lambda i: (0, i)),
-            pl.BlockSpec((batch, width), lambda i: (0, 0)),
-        ]
-        out_specs = pl.BlockSpec((BLOCK, width), lambda i: (i, 0))
-    else:
-        grid, body, scratch = width // CHUNK, grad_columns_kernel, [pltpu.VMEM((height, batch), bf16)]
-        in_specs = [
+    return pl.pallas_call(
+        grad_kernel,
+        grid=(width // CHUNK,),
+        out_shape=jax.ShapeDtypeStruct((height, width), bf16),
+        in_specs=[
             pl.BlockSpec((batch, height), lambda i: (0, 0)),
             pl.BlockSpec((batch, CHUNK), lambda i: (0, i)),
-        ]
-        out_specs = pl.BlockSpec((height, CHUNK), lambda i: (0, i))
-    return pl.pallas_call(
-        body,
-        grid=(grid,),
-        out_shape=jax.ShapeDtypeStruct((height, width), bf16),
-        in_specs=in_specs,
-        out_specs=out_specs,
-        scratch_shapes=scratch,
-        compiler_params=pltpu.CompilerParams(vmem_limit_bytes=48 * 1024 * 1024),
+        ],
+        out_specs=pl.BlockSpec((height, CHUNK), lambda i: (0, i)),
+        scratch_shapes=[pltpu.VMEM((height, batch), bf16)],
+        compiler_params=pltpu.CompilerParams(vmem_limit_bytes=VMEM_BYTES),
         cost_estimate=pl.CostEstimate(
             flops=2 * batch * height * width, bytes_accessed=2 * height * width, transcendentals=0
         ),
@@ -389,8 +416,8 @@
         total = total + lax.ppermute(blocks[k - 1], "row", shift).astype(f32)
     total = total.astype(bf16)
 
-    grad_out_w = weight_grad(act, og, True)
-    grad_in_w = weight_grad(x, hg, False)
+    grad_out_w = weight_grad(act, og)
+    grad_in_w = weight_grad(x, hg)
     return (total[0], total[1], grad_in_w, grad_out_w)
 
 

time: 123 us -> 133 us (1.081); the launches traced: 123 us -> 132 us
  Pallas kernels: 115 us -> 124 us
  local copies, waits for them, and re-layouts: 3.28 us -> 0.73 us
    pallas_call x2, Pallas kernels: 20.3 us -> 26.8 us  [weight_grad(): pl.pallas_call(grad_kernel, grid=(width // CHUNK,), out_shape=jax.ShapeDt...]
    unnamed x10 -> x0, local copies, waits for them, and re-layouts: 2.55 us -> none
    pallas_call x1, Pallas kernels: 95.2 us -> 97.7 us  [layer(): pl.pallas_call(functools.partial(layer_kernel, rows, cols), out_shape=(ja...]
  transfers between devices with their start and end apart: 3 -> 3, of which waited for: 0 -> 0; matrix products, arithmetic and copies ran while one was open for 0% -> 0% of each run, Pallas kernels for 16% -> 20%
where the time goes in v3:
time: 133 us; the launch traced here: 132 us
  Pallas kernels  124 us (93%)
  starting transfers between devices  4.52 us (3%)
  other arithmetic  1.45 us (1%)
    pallas_call x1, Pallas kernels, layer(): pl.pallas_call(functools.partial(layer_kernel, rows, cols), out_shape=(ja...  97.7 us
    pallas_call x2, Pallas kernels, weight_grad(): pl.pallas_call(grad_kernel, grid=(width // CHUNK,), out_shape=jax.ShapeDt...  26.8 us
    ppermute x3, starting transfers between devices, local(): total = total + lax.ppermute(blocks[k - 1], 'row', shift).astype(f32)  4.52 us
  transfers between devices with their start and end apart: 3, of which 0 were waited for; matrix products, arithmetic and copies ran while one was open for 0% of the time, Pallas kernels for 20%

profile of v3, /device:TPU:0, one launch (start us, length us, event | category | flops | bytes accessed | tf_op | source)
XLA Modules:
  0.0 131.8 jit_solution(15491982816351484201)
XLA Ops:
  0.6 97.7 %shard_map.75 = (bf16[192,3072]{1,0:T(8,128)(2,1)}, bf16[192,3072]{1,0:T(8,128)(2,1)}, bf16[192,3072]{1,0:T(8,128)(2,1)}, bf16[192,3072]{1,0:T(8,128)(2,1)}, f32...) custom-call(bf16[24,3072]{1,0:T(8,128)(2,1)} %own_in.1, ...), custom_call_target="tpu_custom_call" | custom-call | flops 14495514624 | bytes 37748736 | tf_op jit(solution)/shard_map/pallas_call | solution.py:333
  98.3 0.8 collective-permute-start
  99.1 1.5 %collective-permute-start.1 = (bf16[2,24,3072]{2,1,0:T(8,128)(2,1)}, bf16[2,24,3072]{2,1,0:T(8,128)(2,1)}, u32[]{:S(2)}, u32[]{:S(2)}) collective-permute-start(bf16[2,24,3072]{2,1,0:T(8,128)(2,1)} %get-tuple-element.14), channel_id=1, source_target_pairs={{0,16},{4,20},{8,24},{12,28},{16,0},{20,4},{24,8},{28,12},{1,17},{... | collective-permute-start | bytes 884744 | tf_op jit(solution)/shard_map/ppermute | solution.py:416
  100.6 2.2 %collective-permute-start.2 = (bf16[2,24,3072]{2,1,0:T(8,128)(2,1)}, bf16[2,24,3072]{2,1,0:T(8,128)(2,1)}, u32[]{:S(2)}, u32[]{:S(2)}) collective-permute-start(bf16[2,24,3072]{2,1,0:T(8,128)(2,1)} %get-tuple-element.15), channel_id=1, source_target_pairs={{0,24},{4,28},{8,0},{12,4},{16,8},{20,12},{24,16},{28,20},{1,25},{... | collective-permute-start | bytes 884744 | tf_op jit(solution)/shard_map/ppermute | solution.py:416
  102.8 13.4 %shard_map.76 = bf16[3072,3072]{1,0:T(8,128)(2,1)} custom-call(bf16[192,3072]{1,0:T(8,128)(2,1)} %get-tuple-element.16.left, bf16[192,3072]{1,0:T(8,128)(2,1)} %get-tuple-element.17.right), custom_call_target="tpu_custom_call" | custom-call | flops 3623878656 | bytes 18874368 | tf_op jit(solution)/shard_map/pallas_call | solution.py:392
  116.2 13.4 %shard_map.77 = bf16[3072,3072]{1,0:T(8,128)(2,1)} custom-call(bf16[192,3072]{1,0:T(8,128)(2,1)} %get-tuple-element.18.left, bf16[192,3072]{1,0:T(8,128)(2,1)} %get-tuple-element.19.right), custom_call_target="tpu_custom_call" | custom-call | flops 3623878656 | bytes 18874368 | tf_op jit(solution)/shard_map/pallas_call | solution.py:392
  129.6 0.0 collective-permute-done
  129.6 0.0 collective-permute-done.1
  129.6 0.0 collective-permute-done.2
  129.6 1.5 %add_convert_fusion = bf16[2,24,3072]{2,1,0:T(8,128)(2,1)S(1)} fusion(bf16[2,24,3072]{2,1,0:T(8,128)(2,1)} %collective-permute-done.2, bf16[2,24,3072]{2,1,0:T(8,128)(2,1)} %collective-permute-done.1, f32[2,24,3072]{2,1,0:T(8,128)} %get-tuple-element.12, bf16[2,24,3072]{2,1,0:T(8,128)(2,1)} %collective-permute-done), kind=kLoop, calls=%fused_computation | loop fusion | flops 1032192 | bytes 1769472 | tf_op jit(solution)/shard_map/convert_element_type | solution.py:417
  131.1 0.7 slice_bitcast_fusion
Async XLA Ops:
  98.3 31.3 %collective-permute-start = (bf16[2,24,3072]{2,1,0:T(8,128)(2,1)}, bf16[2,24,3072]{2,1,0:T(8,128)(2,1)}, u32[]{:S(2)}, u32[]{:S(2)}) collective-permute-start(bf16[2,24,3072]{2,1,0:T(8,128)(2,1)} %get-tuple-element.13), channel_id=1, source_target_pairs={{0,8},{4,12},{8,16},{12,20},{16,24},{20,28},{24,0},{28,4},{1,9},{5... | collective-permute-start | bytes 884744 | tf_op jit(solution)/shard_map/ppermute | solution.py:416
  99.1 30.5 %collective-permute-start.1 = (bf16[2,24,3072]{2,1,0:T(8,128)(2,1)}, bf16[2,24,3072]{2,1,0:T(8,128)(2,1)}, u32[]{:S(2)}, u32[]{:S(2)}) collective-permute-start(bf16[2,24,3072]{2,1,0:T(8,128)(2,1)} %get-tuple-element.14), channel_id=1, source_target_pairs={{0,16},{4,20},{8,24},{12,28},{16,0},{20,4},{24,8},{28,12},{1,17},{... | collective-permute-start | bytes 884744 | tf_op jit(solution)/shard_map/ppermute | solution.py:416
  100.6 29.0 %collective-permute-start.2 = (bf16[2,24,3072]{2,1,0:T(8,128)(2,1)}, bf16[2,24,3072]{2,1,0:T(8,128)(2,1)}, u32[]{:S(2)}, u32[]{:S(2)}) collective-permute-start(bf16[2,24,3072]{2,1,0:T(8,128)(2,1)} %get-tuple-element.15), channel_id=1, source_target_pairs={{0,24},{4,28},{8,0},{12,4},{16,8},{20,12},{24,16},{28,20},{1,25},{... | collective-permute-start | bytes 884744 | tf_op jit(solution)/shard_map/ppermute | solution.py:416

commit v4 on v2

--- a/solution.py
+++ b/solution.py
@@ -11,7 +11,6 @@
 gelu_cubic = 0.044715
 MESH = pl.DeviceIdType.MESH
 CHUNK = 256
-BLOCK = 768
 f32, bf16 = jnp.float32, jnp.bfloat16
 
 
@@ -63,21 +62,24 @@
             pltpu.make_async_copy(w_out.at[cut, :], wout.at[j], w_sem.at[1, j]),
         )
 
+    barrier = pltpu.get_barrier_semaphore()
+    for k in range(1, chips):
+        there = lax.rem(chip + k, chips) * 2 + core
+        pl.semaphore_signal(barrier, inc=1, device_id=(there, col), device_id_type=MESH)
+    pl.semaphore_signal(barrier, inc=1, device_id=(sibling, col), device_id_type=MESH)
+    pl.semaphore_signal(barrier, inc=1, device_id=(row, inner), device_id_type=MESH)
+
+    @pl.when(has_outer)
+    def _():
+        pl.semaphore_signal(barrier, inc=1, device_id=(row, outer), device_id_type=MESH)
+
     @pl.loop(0, chunks)
     def _(j):
         for copy in weight_copies(j):
             copy.start()
 
-    barrier = pltpu.get_barrier_semaphore()
-    for k in range(1, chips):
-        there = lax.rem(chip + k, chips) * 2 + core
-        pl.semaphore_signal(barrier, inc=1, device_id=(there, col), device_id_type=MESH)
-    pl.semaphore_signal(barrier, inc=1, device_id=(sibling, col), device_id_type=MESH)
-    pl.semaphore_signal(barrier, inc=1, device_id=(row, inner), device_id_type=MESH)
-
     @pl.when(has_outer)
     def _():
-        pl.semaphore_signal(barrier, inc=1, device_id=(row, outer), device_id_type=MESH)
         pl.semaphore_wait(barrier, chips + 2)
 
     @pl.when(jnp.logical_not(has_outer))
@@ -336,11 +338,7 @@
     )(inputs, out_grad, w_in, w_out)
 
 
-def grad_rows_kernel(left, right, out):
-    out[...] = contract_first(left[...], right[...]).astype(bf16)
-
-
-def grad_columns_kernel(left, right, out, turned):
+def grad_kernel(left, right, out, turned):
     @pl.when(pl.program_id(0) == 0)
     def _():
         turned[...] = left[...].T
@@ -348,30 +346,19 @@
     out[...] = jnp.dot(turned[...], right[...], preferred_element_type=f32).astype(bf16)
 
 
-def weight_grad(left, right, by_rows):
+def weight_grad(left, right):
     batch, height = left.shape
     width = right.shape[1]
-    if by_rows:
-        grid, body, scratch = height // BLOCK, grad_rows_kernel, []
-        in_specs = [
-            pl.BlockSpec((batch, BLOCK), lambda i: (0, i)),
-            pl.BlockSpec((batch, width), lambda i: (0, 0)),
-        ]
-        out_specs = pl.BlockSpec((BLOCK, width), lambda i: (i, 0))
-    else:
-        grid, body, scratch = width // CHUNK, grad_columns_kernel, [pltpu.VMEM((height, batch), bf16)]
-        in_specs = [
+    return pl.pallas_call(
+        grad_kernel,
+        grid=(width // CHUNK,),
+        out_shape=jax.ShapeDtypeStruct((height, width), bf16),
+        in_specs=[
             pl.BlockSpec((batch, height), lambda i: (0, 0)),
             pl.BlockSpec((batch, CHUNK), lambda i: (0, i)),
-        ]
-        out_specs = pl.BlockSpec((height, CHUNK), lambda i: (0, i))
-    return pl.pallas_call(
-        body,
-        grid=(grid,),
-        out_shape=jax.ShapeDtypeStruct((height, width), bf16),
-        in_specs=in_specs,
-        out_specs=out_specs,
-        scratch_shapes=scratch,
+        ],
+        out_specs=pl.BlockSpec((height, CHUNK), lambda i: (0, i)),
+        scratch_shapes=[pltpu.VMEM((height, batch), bf16)],
         compiler_params=pltpu.CompilerParams(vmem_limit_bytes=48 * 1024 * 1024),
         cost_estimate=pl.CostEstimate(
             flops=2 * batch * height * width, bytes_accessed=2 * height * width, transcendentals=0
@@ -389,8 +376,8 @@
         total = total + lax.ppermute(blocks[k - 1], "row", shift).astype(f32)
     total = total.astype(bf16)
 
-    grad_out_w = weight_grad(act, og, True)
-    grad_in_w = weight_grad(x, hg, False)
+    grad_out_w = weight_grad(act, og)
+    grad_in_w = weight_grad(x, hg)
     return (total[0], total[1], grad_in_w, grad_out_w)
 
 

time: 123 us -> 126 us (1.024)
  Pallas kernels: 115 us -> 118 us
    pallas_call x2, Pallas kernels: 20.3 us -> 22.9 us  [weight_grad(): pl.pallas_call(grad_kernel, grid=(width // CHUNK,), out_shape=jax.ShapeDt...]
  transfers between devices with their start and end apart: 3 -> 3, of which waited for: 0 -> 0; matrix products, arithmetic and copies ran while one was open for 0% -> 0% of each run, Pallas kernels for 16% -> 18%
where the time goes in v4:
time: 126 us
  Pallas kernels  118 us (94%)
  starting transfers between devices  3.66 us (3%)
  local copies, waits for them, and re-layouts  3.28 us (3%)
    pallas_call x1, Pallas kernels, layer(): pl.pallas_call(functools.partial(layer_kernel, rows, cols), out_shape=(ja...  95.1 us
    pallas_call x2, Pallas kernels, weight_grad(): pl.pallas_call(grad_kernel, grid=(width // CHUNK,), out_shape=jax.ShapeDt...  22.9 us
    ppermute x3, starting transfers between devices, local(): total = total + lax.ppermute(blocks[k - 1], 'row', shift).astype(f32)  3.66 us
    unnamed x10, local copies, waits for them, and re-layouts  2.55 us
  transfers between devices with their start and end apart: 3, of which 0 were waited for; matrix products, arithmetic and copies ran while one was open for 0% of the time, Pallas kernels for 18%

profile of v4, /device:TPU:0, one launch (start us, length us, event | category | flops | bytes accessed | tf_op | source)
XLA Modules:
  0.0 125.7 jit_solution(5776027548823490396)
XLA Ops:
  0.6 95.1 %shard_map.75 = (bf16[192,3072]{1,0:T(8,128)(2,1)}, bf16[192,3072]{1,0:T(8,128)(2,1)}, bf16[192,3072]{1,0:T(8,128)(2,1)}, bf16[192,3072]{1,0:T(8,128)(2,1)}, f32...) custom-call(bf16[24,3072]{1,0:T(8,128)(2,1)} %own_in.1, ...), custom_call_target="tpu_custom_call" | custom-call | flops 14495514624 | bytes 37748736 | tf_op jit(solution)/shard_map/pallas_call | solution.py:293
  95.8 0.0 copy-start
  95.8 0.0 copy-start.1
  95.8 0.8 collective-permute-start
  96.6 1.8 %collective-permute-start.1 = (bf16[2,24,3072]{2,1,0:T(8,128)(2,1)}, bf16[2,24,3072]{2,1,0:T(8,128)(2,1)S(1)}, u32[]{:S(2)}, u32[]{:S(2)}) collective-permute-start(bf16[2,24,3072]{2,1,0:T(8,128)(2,1)} %get-tuple-element.14), channel_id=1, source_target_pairs={{0,16},{4,20},{8,24},{12,28},{16,0},{20,4},{24,8},{28,12},{1,17},{... | collective-permute-start | bytes 884744 | tf_op jit(solution)/shard_map/ppermute | solution.py:376
  98.4 1.0 collective-permute-start.2
  99.4 0.0 copy-start.2
  99.4 1.3 %copy-done.2 = bf16[192,3072]{1,0:T(8,128)(2,1)S(1)} copy-done((bf16[192,3072]{1,0:T(8,128)(2,1)S(1)}, bf16[192,3072]{1,0:T(8,128)(2,1)}, u32[]{:S(2)}) %copy-start.2) | copy-done | bytes 1179672
  100.7 0.0 copy-start.3
  100.7 1.3 %copy-done.3 = bf16[192,3072]{1,0:T(8,128)(2,1)S(1)} copy-done((bf16[192,3072]{1,0:T(8,128)(2,1)S(1)}, bf16[192,3072]{1,0:T(8,128)(2,1)}, u32[]{:S(2)}) %copy-start.3) | copy-done | bytes 1179672
  102.0 0.0 copy-start.4
  102.0 11.4 %shard_map.76 = bf16[3072,3072]{1,0:T(8,128)(2,1)} custom-call(bf16[192,3072]{1,0:T(8,128)(2,1)S(1)} %copy-done.2, bf16[192,3072]{1,0:T(8,128)(2,1)S(1)} %copy-done.3), custom_call_target="tpu_custom_call" | custom-call | flops 3623878656 | bytes 18874368 | tf_op jit(solution)/shard_map/pallas_call | solution.py:352
  113.4 0.0 copy-done
  113.4 0.0 copy-done.1
  113.4 11.4 %shard_map.77 = bf16[3072,3072]{1,0:T(8,128)(2,1)} custom-call(bf16[192,3072]{1,0:T(8,128)(2,1)S(1)} %copy-done.1, bf16[192,3072]{1,0:T(8,128)(2,1)S(1)} %copy-done), custom_call_target="tpu_custom_call" | custom-call | flops 3623878656 | bytes 18874368 | tf_op jit(solution)/shard_map/pallas_call | solution.py:352
  124.8 0.0 collective-permute-done
  124.8 0.0 collective-permute-done.1
  124.8 0.0 collective-permute-done.2
  124.9 0.0 copy-done.4
  124.9 0.1 add_convert_fusion
  125.0 0.7 slice_bitcast_fusion
Async XLA Ops:
  95.8 17.7 %copy-start = (bf16[192,3072]{1,0:T(8,128)(2,1)S(1)}, bf16[192,3072]{1,0:T(8,128)(2,1)}, u32[]{:S(2)}) copy-start(bf16[192,3072]{1,0:T(8,128)(2,1)} %get-tuple-element.19.right) | copy-start | bytes 3538948
  95.8 17.6 %copy-start.1 = (bf16[192,3072]{1,0:T(8,128)(2,1)S(1)}, bf16[192,3072]{1,0:T(8,128)(2,1)}, u32[]{:S(2)}) copy-start(bf16[192,3072]{1,0:T(8,128)(2,1)} %get-tuple-element.18.left) | copy-start | bytes 3538948
  95.8 29.1 %collective-permute-start = (bf16[2,24,3072]{2,1,0:T(8,128)(2,1)}, bf16[2,24,3072]{2,1,0:T(8,128)(2,1)S(1)}, u32[]{:S(2)}, u32[]{:S(2)}) collective-permute-start(bf16[2,24,3072]{2,1,0:T(8,128)(2,1)} %get-tuple-element.13), channel_id=1, source_target_pairs={{0,8},{4,12},{8,16},{12,20},{16,24},{20,28},{24,0},{28,4},{1,9},{5... | collective-permute-start | bytes 884744 | tf_op jit(solution)/shard_map/ppermute | solution.py:376
  96.6 28.2 %collective-permute-start.1 = (bf16[2,24,3072]{2,1,0:T(8,128)(2,1)}, bf16[2,24,3072]{2,1,0:T(8,128)(2,1)S(1)}, u32[]{:S(2)}, u32[]{:S(2)}) collective-permute-start(bf16[2,24,3072]{2,1,0:T(8,128)(2,1)} %get-tuple-element.14), channel_id=1, source_target_pairs={{0,16},{4,20},{8,24},{12,28},{16,0},{20,4},{24,8},{28,12},{1,17},{... | collective-permute-start | bytes 884744 | tf_op jit(solution)/shard_map/ppermute | solution.py:376
  98.4 26.4 %collective-permute-start.2 = (bf16[2,24,3072]{2,1,0:T(8,128)(2,1)}, bf16[2,24,3072]{2,1,0:T(8,128)(2,1)S(1)}, u32[]{:S(2)}, u32[]{:S(2)}) collective-permute-start(bf16[2,24,3072]{2,1,0:T(8,128)(2,1)} %get-tuple-element.15), channel_id=1, source_target_pairs={{0,24},{4,28},{8,0},{12,4},{16,8},{20,12},{24,16},{28,20},{1,25},{... | collective-permute-start | bytes 884744 | tf_op jit(solution)/shard_map/ppermute | solution.py:376
  99.4 1.3 %copy-start.2 = (bf16[192,3072]{1,0:T(8,128)(2,1)S(1)}, bf16[192,3072]{1,0:T(8,128)(2,1)}, u32[]{:S(2)}) copy-start(bf16[192,3072]{1,0:T(8,128)(2,1)} %get-tuple-element.16.left) | copy-start | bytes 3538948
  100.7 1.3 %copy-start.3 = (bf16[192,3072]{1,0:T(8,128)(2,1)S(1)}, bf16[192,3072]{1,0:T(8,128)(2,1)}, u32[]{:S(2)}) copy-start(bf16[192,3072]{1,0:T(8,128)(2,1)} %get-tuple-element.17.right) | copy-start | bytes 3538948
  102.0 22.9 %copy-start.4 = (f32[2,24,3072]{2,1,0:T(8,128)S(1)}, f32[2,24,3072]{2,1,0:T(8,128)}, u32[]{:S(2)}) copy-start(f32[2,24,3072]{2,1,0:T(8,128)} %get-tuple-element.12) | copy-start | bytes 1769476
